TPU v7x, 256 devices: a whole 4x4x8 slice. The times are simulated.
256 devices in a mesh: ev: 32 (over y, z_lo, core), st: 8 (over z_hi, x).
Axes of the slice: x: 4, y: 4, z: 8 (z_hi: 2, z_lo: 4; z = z_hi * 4 + z_lo), core: 2. Of those that a mesh axis runs over, the one named last changes fastest.
Arguments:
- strain: bfloat16 [2, 6, 512, 8192], P(None, None, 'ev'), may hold values from -0.048339844 to 0.048339844
- green: bfloat16 [2, 3, 1024, 6, 8192], P(None, None, 'st', None, 'ev'), may hold values from -6 to 6
- weights: bfloat16 [2, 3, 512, 1024], P(None, None, 'ev', 'st'), may hold values from -0.078125 to 0.078125
- mask: int32 [512, 1024], P('ev', 'st'), may hold values 0 or 1
Outputs:
- kernels: float32 [2, 8192], P(None, ('ev', 'st'))
All inputs are finite; a program needn't handle non-finite values. No bound on the sum of `mask` on one device may be relied on, other than what follows from the above.
Results may differ from a plain program's by a relative error of at most 0.0003.
Values may be sent and summed in bfloat16 or wider, within the bound.
A program may use at most 128 MiB of HBM per device.

v0:
```python
import jax
import jax.numpy as jnp
from jax import lax
from jax.sharding import Mesh
from jax.sharding import PartitionSpec as P

EV = ("ev_0", "ev_1", "ev_2")
EV_ST = ("ev_0", "ev_1", "ev_2", "st")


def in_blocks(x, dim, count):
    before, after = (x.shape[:dim], x.shape[dim + 1 :])
    return jnp.moveaxis(x.reshape(*before, count, -1, *after), dim, 0)


def joined_along(blocks, dim):
    blocks = jnp.moveaxis(blocks, 0, dim)
    shape = blocks.shape
    return blocks.reshape(*shape[:dim], shape[dim] * shape[dim + 1], *shape[dim + 2 :])


def turned_blocks(blocks, axes, sequence):
    shape = [lax.axis_size(a) for a in axes]
    blocks = blocks.reshape(*shape, *blocks.shape[1:])
    for k in sequence:
        blocks = lax.all_to_all(blocks, axes[k], split_axis=k, concat_axis=k, tiled=True)
    return blocks.reshape(-1, *blocks.shape[len(axes) :])


def core_and_chips(x, groups, sequence, split_dim, concat_dim):
    count = lax.axis_size(groups[0]) * lax.axis_size(groups[1])
    blocks = in_blocks(x, split_dim, count)
    return joined_along(turned_blocks(blocks, groups, sequence), concat_dim)


def sent_to_all(x, axis):
    count = lax.axis_size(axis)
    return lax.all_to_all(jnp.broadcast_to(x[None], (count, *x.shape)), axis, 0, 0, tiled=True)


def gather_directly(x, axis, dim):
    blocks = sent_to_all(x, axis)
    return joined_along(blocks, dim)


def sent_and_summed(x, axis, dim):
    count = lax.axis_size(axis)
    blocks = lax.all_to_all(in_blocks(x, dim, count), axis, 0, 0, tiled=True)
    return jnp.sum(blocks, axis=0)


def local(strain, green, weights, mask):
    masked = weights * mask.astype(jnp.bfloat16)[None, None]
    cells_dev = green.shape[4]
    station_count = green.shape[2]
    strain_all = core_and_chips(strain, (("ev_0", "ev_1"), "ev_2"), (1, 0), 3, 2)
    green_flat = green.reshape(2, 3, station_count, 6 * cells_dev)
    voigt = jnp.array([1.0, 1.0, 1.0, 2.0, 2.0, 2.0], jnp.float32)
    weight_rows = gather_directly(masked, EV, 2)
    row_count = weight_rows.shape[2]
    products = jnp.einsum(
        "rfps,qfsn->rqpn", weight_rows, green_flat, preferred_element_type=jnp.float32
    )
    held_real = (products[0, 0] - products[1, 1]).reshape(row_count, 6, cells_dev)
    held_imag = (products[0, 1] + products[1, 0]).reshape(row_count, 6, cells_dev)
    strain_rows = strain_all.astype(jnp.float32)
    strain_real = jnp.swapaxes(strain_rows[0], 0, 1)
    strain_imag = jnp.swapaxes(strain_rows[1], 0, 1)
    trace_term = jnp.sum(
        strain_real[:, :3].sum(1) * held_real[:, :3].sum(1)
        - strain_imag[:, :3].sum(1) * held_imag[:, :3].sum(1),
        axis=0,
    )
    shear_term = jnp.sum(
        (strain_real * held_real - strain_imag * held_imag) * voigt[None, :, None], axis=(0, 1)
    )
    partial_value = jnp.stack([trace_term, shear_term])
    return sent_and_summed(partial_value, "st", 1)


def solution(mesh):
    torus = Mesh(mesh.devices.reshape(4, 4, 2, mesh.shape["st"]), ("ev_0", "ev_1", "ev_2", "st"))
    return jax.shard_map(
        local,
        mesh=torus,
        in_specs=(
            P(None, None, EV, None),
            P(None, None, "st", None, EV),
            P(None, None, EV, "st"),
            P(EV, "st"),
        ),
        out_specs=P(None, EV_ST),
        check_vma=False,
    )
```

profile of v0, /device:TPU:1, one launch (start us, length us, event | category | flops | bytes accessed | tf_op | source)
XLA Modules:
  0.0 152.7 jit_solution(5297103895057971065)
XLA Ops:
  0.0 2.8 %copy.66 = bf16[24,8,32,256]{3,2,1,0:T(8,128)(2,1)S(1)} copy(bf16[24,8,32,256]{3,1,2,0:T(8,128)(2,1)} %bitcast.49) | data formatting | bytes 6291456
  2.8 1.8 %copy.49 = bf16[32,2,6,16,256]{4,3,2,1,0:T(8,128)(2,1)S(1)} copy(bf16[32,2,6,16,256]{4,0,3,2,1:T(8,128)(2,1)S(1)} %bitcast.47) | data formatting | bytes 6291456 | tf_op jit(solution)/shard_map/transpose | solution.py:13
  4.6 2.1 %copy.50 = bf16[16,2,2,6,16,256]{5,4,0,3,2,1:T(8,128)(2,1)} copy(bf16[16,2,2,6,16,256]{5,4,3,2,1,0:T(8,128)(2,1)S(1)} %bitcast.46) | data formatting | bytes 6291456 | tf_op jit(solution)/shard_map/reshape | solution.py:24
  6.7 0.0 copy-start.3
  6.7 0.0 copy-start.2
  6.7 7.3 %all-to-all-start = ((bf16[16,2,2,6,16,256]{5,4,0,3,2,1:T(8,128)(2,1)}), bf16[16,2,2,6,16,256]{5,4,0,3,2,1:T(8,128)(2,1)S(1)}, u32[]{:S(2)}, u32[]{:S(2)}) async-start(bf16[16,2,2,6,16,256]{5,4,0,3,2,1:T(8,128)(2,1)} %copy.50), calls=%async_computation | async-start | bytes 6291456 | tf_op jit(solution)/shard_map/all_to_all | solution.py:26
  14.0 0.0 copy-done.3
  14.0 0.0 copy-done.2
  14.0 3.2 %all-to-all-done = bf16[16,2,2,6,16,256]{5,4,0,3,2,1:T(8,128)(2,1)S(1)} async-done(((bf16[16,2,2,6,16,256]{5,4,0,3,2,1:T(8,128)(2,1)}), bf16[16,2,2,6,16,256]{5,4,0,3,2,1:T(8,128)(2,1)S(1)}, u32[]{:S(2)}, u32[]{:S(2)}) %all-to-all-start) | async-done | bytes 3145760 | tf_op jit(solution)/shard_map/all_to_all | solution.py:26
  17.2 1.0 broadcast_in_dim.2
  18.2 7.4 %all-to-all-start.2 = ((bf16[32,2,3,16,128]{4,3,2,1,0:T(8,128)(2,1)}), bf16[32,2,3,16,128]{4,3,2,1,0:T(8,128)(2,1)}, u32[]{:S(2)}, u32[]{:S(2)}) async-start(bf16[32,2,3,16,128]{4,3,2,1,0:T(8,128)(2,1)} %broadcast_in_dim.2), calls=%async_computation.2 | async-start | bytes 1572864 | tf_op jit(solution)/shard_map/all_to_all | solution.py:38
  25.6 2.2 %copy.51 = bf16[16,2,2,6,16,256]{5,4,1,3,2,0:T(8,128)(2,1)} copy(bf16[16,2,2,6,16,256]{5,4,0,3,2,1:T(8,128)(2,1)S(1)} %all-to-all-done) | data formatting | bytes 6291456 | tf_op jit(solution)/shard_map/all_to_all | solution.py:26
  27.8 20.2 %all-to-all-done.2 = bf16[32,2,3,16,128]{4,3,2,1,0:T(8,128)(2,1)} async-done(((bf16[32,2,3,16,128]{4,3,2,1,0:T(8,128)(2,1)}), bf16[32,2,3,16,128]{4,3,2,1,0:T(8,128)(2,1)}, u32[]{:S(2)}, u32[]{:S(2)}) %all-to-all-start.2) | async-done | bytes 786464 | tf_op jit(solution)/shard_map/all_to_all | solution.py:38
  48.0 4.7 %all-to-all-start.1 = ((bf16[16,2,2,6,16,256]{5,4,1,3,2,0:T(8,128)(2,1)}), bf16[16,2,2,6,16,256]{5,4,1,3,2,0:T(8,128)(2,1)}, u32[]{:S(2)}, u32[]{:S(2)}) async-start(bf16[16,2,2,6,16,256]{5,4,1,3,2,0:T(8,128)(2,1)} %copy.51), calls=%async_computation.1 | async-start | bytes 6291456 | tf_op jit(solution)/shard_map/all_to_all | solution.py:26
  52.7 3.1 %copy.54 = bf16[2,3,128,6,256]{2,4,3,1,0:T(8,128)(2,1)S(1)} copy(bf16[2,3,128,6,256]{4,2,3,1,0:T(8,128)(2,1)} %param.6) | data formatting | bytes 4718592 | tf_op args[1]
  55.7 1.3 copy.53
  57.0 3.5 %convolution_bitcast_fusion = f32[2,2,512,1536]{3,2,1,0:T(8,128)S(1)} fusion(bf16[2,3,512,128,1]{3,2,1,4,0:T(8,128)(2,1)S(1)} %bitcast.50, bf16[2,3,128,1536,1]{2,3,1,0,4:T(8,128)(2,1)S(1)} %bitcast.48), kind=kOutput, calls=%fused_computation | convolution fusion | flops 2415919104 | bytes 15728640 | tf_op jit(solution)/shard_map/rfps,qfsn->rqpn/dot_general | solution.py:61
  60.5 4.1 %slice_subtract_fusion = (f32[1,1,512,1536]{3,2,1,0:T(8,128)}, f32[1,1,512,1536]{3,2,1,0:T(8,128)}) fusion(f32[2,2,512,1536]{3,2,1,0:T(8,128)S(1)} %convolution_bitcast_fusion), kind=kLoop, calls=%fused_computation.2 | loop fusion | flops 1572864 | bytes 18874368 | tf_op jit(solution)/shard_map/sub | solution.py:64
  64.5 2.4 %copy.58 = f32[1,1,512,1536]{2,3,1,0:T(8,128)S(1)} copy(f32[1,1,512,1536]{3,2,1,0:T(8,128)} %get-tuple-element.6) | data formatting | bytes 6291456 | tf_op jit(solution)/shard_map/add | solution.py:65
  66.9 2.4 %copy.61 = f32[512,6,256]{2,0,1:T(8,128)} copy(f32[512,6,256]{0,2,1:T(8,128)S(1)} %bitcast.38) | data formatting | bytes 6291456 | tf_op jit(solution)/shard_map/add | solution.py:65
  69.3 3.6 %copy.56 = f32[1,1,512,1536]{2,3,1,0:T(8,128)} copy(f32[1,1,512,1536]{3,2,1,0:T(8,128)} %get-tuple-element.5) | data formatting | bytes 6291456 | tf_op jit(solution)/shard_map/sub | solution.py:64
  72.9 3.5 %copy.60 = f32[512,6,256]{2,0,1:T(8,128)} copy(f32[512,6,256]{0,2,1:T(8,128)} %bitcast.40) | data formatting | bytes 6291456 | tf_op jit(solution)/shard_map/sub | solution.py:64
  76.4 0.9 slice_reduce_fusion
  77.3 1.2 copy.59
  78.6 1.6 %slice_reduce_fusion.2 = f32[512,256]{0,1:T(8,128)S(1)} fusion(f32[512,6,256]{0,2,1:T(8,128)} %bitcast.41), kind=kLoop, calls=%fused_computation.6 | loop fusion | flops 262144 | bytes 2097152 | tf_op jit(solution)/shard_map/reduce_sum | solution.py:70
  80.2 0.2 copy.57
  80.4 47.3 %all-to-all-done.1 = bf16[16,2,2,6,16,256]{5,4,1,3,2,0:T(8,128)(2,1)} async-done(((bf16[16,2,2,6,16,256]{5,4,1,3,2,0:T(8,128)(2,1)}), bf16[16,2,2,6,16,256]{5,4,1,3,2,0:T(8,128)(2,1)}, u32[]{:S(2)}, u32[]{:S(2)}) %all-to-all-start.1) | async-done | bytes 3145760 | tf_op jit(solution)/shard_map/all_to_all | solution.py:26
  127.7 2.8 %copy.52 = f32[16,2,2,6,16,256]{5,4,1,0,3,2:T(8,128)S(1)} copy(bf16[16,2,2,6,16,256]{5,4,1,3,2,0:T(8,128)(2,1)} %all-to-all-done.1) | data formatting | bytes 9437184 | tf_op jit(solution)/shard_map/convert_element_type | solution.py:66
  130.4 0.0 copy-start.1
  130.4 0.7 fusion
  131.2 0.0 copy-start
  131.2 0.0 copy-start.4
  131.2 0.2 slice_reduce_fusion.1
  131.4 0.9 copy-done.1
  132.3 1.1 copy-done
  133.5 0.0 copy-done.4
  133.5 1.6 %multiply_reduce_fusion = f32[256]{0:T(256)S(1)} fusion(f32[512,6,256]{2,0,1:T(8,128)S(1)} %bitcast.45, f32[512,6,256]{2,0,1:T(8,128)S(1)} %copy-done, f32[512,6,256]{2,0,1:T(8,128)S(1)} %bitcast.43, f32[512,6,256]{2,0,1:T(8,128)S(1)} %copy-done.1, f32[6]{0:T(128)S(1)} %copy-done.4), kind=kLoop, calls=%fused_computation.3 | loop fusion | flops 3931904 | bytes 12583960 | tf_op jit(solution)/shard_map/reduce_sum | solution.py:74
  135.1 0.1 stack.10
  135.1 0.2 subtract_reduce_fusion
  135.3 0.1 stack.9
  135.4 16.7 %all_to_all.20 = f32[8,2,32]{2,1,0:T(2,128)S(1)} all-to-all(f32[8,2,32]{2,1,0:T(2,128)S(1)} %maximum_bitcast_fusion), channel_id=1, replica_groups=mesh['ev_0'=4,'ev_1'=4,'ev_2'=2,'st'=8] {'st'}, dimensions={0} | all-to-all | bytes 4096 | tf_op jit(solution)/shard_map/all_to_all | solution.py:48
  152.1 0.6 reduce_sum.69
  (3 shorter events, 0.0 us)
Async XLA Ops:
  6.7 7.3 %copy-start.3 = (s32[16,128]{1,0:T(8,128)S(1)}, s32[16,128]{1,0:T(8,128)}, u32[]{:S(2)}) copy-start(s32[16,128]{1,0:T(8,128)} %param.8) | copy-start | bytes 24580
  6.7 7.3 %copy-start.2 = (bf16[2,3,16,128]{3,2,1,0:T(8,128)(2,1)S(1)}, bf16[2,3,16,128]{3,2,1,0:T(8,128)(2,1)}, u32[]{:S(2)}) copy-start(bf16[2,3,16,128]{3,2,1,0:T(8,128)(2,1)} %param.7) | copy-start | bytes 73732
  6.7 10.6 %all-to-all-start = ((bf16[16,2,2,6,16,256]{5,4,0,3,2,1:T(8,128)(2,1)}), bf16[16,2,2,6,16,256]{5,4,0,3,2,1:T(8,128)(2,1)S(1)}, u32[]{:S(2)}, u32[]{:S(2)}) async-start(bf16[16,2,2,6,16,256]{5,4,0,3,2,1:T(8,128)(2,1)} %copy.50), calls=%async_computation | async-start | bytes 6291456 | tf_op jit(solution)/shard_map/all_to_all | solution.py:26
  18.2 29.8 %all-to-all-start.2 = ((bf16[32,2,3,16,128]{4,3,2,1,0:T(8,128)(2,1)}), bf16[32,2,3,16,128]{4,3,2,1,0:T(8,128)(2,1)}, u32[]{:S(2)}, u32[]{:S(2)}) async-start(bf16[32,2,3,16,128]{4,3,2,1,0:T(8,128)(2,1)} %broadcast_in_dim.2), calls=%async_computation.2 | async-start | bytes 1572864 | tf_op jit(solution)/shard_map/all_to_all | solution.py:38
  48.0 79.7 %all-to-all-start.1 = ((bf16[16,2,2,6,16,256]{5,4,1,3,2,0:T(8,128)(2,1)}), bf16[16,2,2,6,16,256]{5,4,1,3,2,0:T(8,128)(2,1)}, u32[]{:S(2)}, u32[]{:S(2)}) async-start(bf16[16,2,2,6,16,256]{5,4,1,3,2,0:T(8,128)(2,1)} %copy.51), calls=%async_computation.1 | async-start | bytes 6291456 | tf_op jit(solution)/shard_map/all_to_all | solution.py:26
  130.4 1.9 %copy-start.1 = (f32[512,6,256]{2,0,1:T(8,128)S(1)}, f32[512,6,256]{2,0,1:T(8,128)}, u32[]{:S(2)}) copy-start(f32[512,6,256]{2,0,1:T(8,128)} %copy.60) | copy-start | bytes 9437188
  131.2 2.3 %copy-start = (f32[512,6,256]{2,0,1:T(8,128)S(1)}, f32[512,6,256]{2,0,1:T(8,128)}, u32[]{:S(2)}) copy-start(f32[512,6,256]{2,0,1:T(8,128)} %copy.61) | copy-start | bytes 9437188
  131.2 2.3 %copy-start.4 = (f32[6]{0:T(128)S(1)}, f32[6]{0:T(128)}, u32[]{:S(2)}) copy-start(f32[6]{0:T(128)} %constant.4.clone) | copy-start | bytes 76
where the time goes:
time: 154 us; the launch traced here: 153 us
  waiting for transfers between devices  70.7 us (46%)
  local copies, waits for them, and re-layouts  33.1 us (21%)
  starting transfers between devices  19.3 us (13%)
  blocking collectives  16.7 us (11%)
  other arithmetic  9.18 us (6%)
  matrix products  3.47 us (2%)
    all_to_all x2, waiting for transfers between devices, turned_blocks(): lax.all_to_all(blocks, axes[k], split_axis=k, concat_axis=k, tiled=True)  50.5 us
    all_to_all x1, waiting for transfers between devices, sent_to_all(): lax.all_to_all(jnp.broadcast_to(x[None], (count, *x.shape)), axis, 0, 0,...  20.2 us
    all_to_all x1, blocking collectives, sent_and_summed(): blocks = lax.all_to_all(in_blocks(x, dim, count), axis, 0, 0, tiled=True)  16.7 us
    all_to_all x2, starting transfers between devices, turned_blocks(): lax.all_to_all(blocks, axes[k], split_axis=k, concat_axis=k, tiled=True)  12 us
    unnamed x12, local copies, waits for them, and re-layouts  7.92 us
    all_to_all x1, starting transfers between devices, sent_to_all(): lax.all_to_all(jnp.broadcast_to(x[None], (count, *x.shape)), axis, 0, 0,...  7.37 us
    sub x2, local copies, waits for them, and re-layouts, local(): products[0, 0] - products[1, 1]  7.06 us
    add x2, local copies, waits for them, and re-layouts, local(): products[0, 1] + products[1, 0]  4.79 us
  transfers between devices with their start and end apart: 3, of which 3 were waited for; matrix products, arithmetic and copies ran while one was open for 20% of the time, Pallas kernels for 0%

commit v1 on v0

v1 whole, which is shorter than its diff:
```python
import jax
import jax.numpy as jnp
from jax import lax
from jax.experimental import pallas as pl
from jax.experimental.pallas import tpu as pltpu
from jax.sharding import PartitionSpec as P

MESH = pl.DeviceIdType.MESH
OFF_AXIS = (1, 3, 2)
GROUPS = tuple((dc, dy) for dy in OFF_AXIS for dc in (0, 1))


def kernel(strain, green, weights, mask, out, sbuf, wbuf, gs, lhs, held, acc, kbuf, krx,
           lsem, ssem, r_s, r_x, r_wz, r_wy, r_wc, r_k):
    ev, st = lax.axis_index("ev"), lax.axis_index("st")
    y, zl, c = ev // 8, (ev // 2) % 4, ev % 2
    zh, x = st // 4, st % 4
    z = zh * 4 + zl

    def device(x_, y_, z_, c_):
        x_, y_, z_ = (x_ + 4) % 4, (y_ + 4) % 4, (z_ + 8) % 8
        return ((y_ * 4 + z_ % 4) * 2 + c_, (z_ // 4) * 4 + x_)

    def far(dz, core):
        return {0: 0, 1: 1, 3: -1}[dz] if dz != 2 else 2 - 4 * core

    def in_half(dz):
        return zh * 4 + (zl + dz) % 4

    sends = []

    def send(src, dst, recv_sem, to):
        copy = pltpu.make_async_remote_copy(
            src_ref=src, dst_ref=dst, send_sem=ssem.at[len(sends)], recv_sem=recv_sem,
            device_id=to, device_id_type=MESH)
        copy.start()
        sends.append(copy)
        return copy

    load_green = [
        pltpu.make_async_copy(green.at[k], gs.at[:, pl.ds(k * 128, 128), :], lsem.at[1 + k]) for k in range(6)]
    for copy in load_green:
        copy.start()

    def cells(ev_):
        return pl.ds(pl.multiple_of(ev_ * 256, 256), 256)

    load_own = pltpu.make_async_copy(strain.at[:, :, cells(ev)], sbuf.at[0, 0, 0], lsem.at[0])
    load_own.start()

    barrier = pltpu.get_barrier_semaphore()
    senders = [device(x, y, z, 1 - c)]
    for dy in range(4):
        for dz in range(4):
            if dy or dz:
                for core in (0, 1):
                    senders.append(device(x, y - dy, z - far(dz, c), core))
    for dz in (1, 2, 3):
        senders.append(device(x, y, in_half(4 - dz), c))
    for dx in range(4):
        for dh in (0, 4):
            if dx or dh:
                senders.append(device(x + dx, y, z + dh, c))
    for d in senders:
        pl.semaphore_signal(barrier, inc=1, device_id=d, device_id_type=MESH)
    wbuf[0, 0, 0] = weights[...] * mask[...].astype(jnp.bfloat16)[None]
    pl.semaphore_wait(barrier, len(senders))

    wz = [send(wbuf.at[0, 0, 0], wbuf.at[0, 0, dz], r_wz.at[dz], device(x, y, in_half(dz), c)) for dz in (1, 2, 3)]

    mine = pl.ds(3 * x, 3)
    def strain_to(dy, dz, dc, slabs):
        core = c if dc == 0 else 1 - c
        to = device(x, y + dy, z + far(dz, core), core)
        return send(strain.at[slabs, :, cells(to[0])], sbuf.at[dc, dy, dz, slabs], r_s.at[dc, dy, dz], to)

    quarters = {}
    for dc, dy in GROUPS:
        quarters[dc, dy] = [strain_to(dy, dz, dc, mine) for dz in (1, 2, 3)]
    whole = pl.ds(0, 12)
    direct = [strain_to(0, 0, 1, whole)]
    for dy, dz in ((1, 0), (0, 1), (3, 0), (0, 3), (2, 0), (0, 2)):
        for dc in (0, 1):
            direct.append(strain_to(dy, dz, dc, whole))

    for copy in wz:
        copy.wait_recv()
    wy = [send(wbuf.at[0, 0], wbuf.at[0, dy], r_wy.at[dy], device(x, y + dy, z, c)) for dy in (1, 3, 2)]

    right, left = device(x + 1, y, z, c), device(x - 1, y, z, c)

    def part(dc, dy, of_x):
        return sbuf.at[dc, dy, pl.ds(1, 3), pl.ds(3 * ((of_x + 4) % 4), 3)]

    to_right, to_left, relays = {}, {}, {}
    for g, (dc, dy) in enumerate(GROUPS):
        for copy in quarters[dc, dy]:
            copy.wait_recv()
        p = part(dc, dy, x)
        to_right[g] = send(p, p, r_x.at[0, g], right)
        to_left[g] = send(p, p, r_x.at[1, g], left)

    for copy in wy:
        copy.wait_recv()
    wc = send(wbuf.at[0], wbuf.at[1], r_wc.at[0], device(x, y, z, 1 - c))

    def relay(g):
        dc, dy = GROUPS[g]
        if dc == 0:
            to_right[g].wait_recv()
            p = part(dc, dy, x - 1)
            relays[g] = send(p, p, r_x.at[2, g], right)
        else:
            to_left[g].wait_recv()
            p = part(dc, dy, x + 1)
            relays[g] = send(p, p, r_x.at[2, g], left)

    relay(0)
    relay(1)
    wc.wait_recv()
    all_w = wbuf.reshape(32, 6, 16, 128)
    for f in range(3):
        real = all_w[:, f].reshape(512, 128)
        imag = all_w[:, 3 + f].reshape(512, 128)
        lhs[0:512, f * 128:(f + 1) * 128] = real
        lhs[0:512, 384 + f * 128:384 + (f + 1) * 128] = -imag
        lhs[512:1024, f * 128:(f + 1) * 128] = imag
        lhs[512:1024, 384 + f * 128:384 + (f + 1) * 128] = real

    def multiply(v, _):
        held[v] = jnp.dot(lhs[...], gs[v], preferred_element_type=jnp.float32)
        return 0

    for copy in load_green:
        copy.wait()
    lax.fori_loop(0, 3, multiply, 0)
    relay(2)
    relay(3)
    lax.fori_loop(3, 6, multiply, 0)
    relay(4)
    relay(5)

    acc[...] = jnp.zeros_like(acc)

    def add_up(slot):
        dc, dy, dz = slot
        row = (dc * 16 + dy * 4 + dz) * 16
        s = sbuf[dc, dy, dz].astype(jnp.float32)
        hr = [held[v, pl.ds(row, 16), :] for v in range(6)]
        hi = [held[v, pl.ds(512 + row, 16), :] for v in range(6)]
        trace = (s[0] + s[1] + s[2]) * (hr[0] + hr[1] + hr[2]) - (s[6] + s[7] + s[8]) * (hi[0] + hi[1] + hi[2])
        normal = sum(s[v] * hr[v] - s[6 + v] * hi[v] for v in range(3))
        shear = sum(s[v] * hr[v] - s[6 + v] * hi[v] for v in range(3, 6))
        acc[0] += trace
        acc[1] += normal + 2.0 * shear

    load_own.wait()
    add_up((0, 0, 0))
    for copy in direct:
        copy.wait_recv()
    add_up((1, 0, 0))
    for dy, dz in ((1, 0), (0, 1), (3, 0), (0, 3), (2, 0), (0, 2)):
        for dc in (0, 1):
            add_up((dc, dy, dz))
    for g, (dc, dy) in enumerate(GROUPS):
        if dc == 0:
            to_left[g].wait_recv()
        else:
            to_right[g].wait_recv()
        relays[g].wait_recv()
        for dz in (1, 2, 3):
            add_up((dc, dy, dz))

    total = acc[...].sum(axis=1)
    kbuf[0, 0:2] = total[:, 0:128]
    kbuf[1, 0:2] = total[:, 128:256]
    shares = []
    for dx in range(4):
        for dh in (0, 1):
            if dx or dh:
                h = (zh + dh) % 2
                shares.append(send(kbuf.at[h], krx.at[dx * 2 + dh], r_k.at[dx * 2 + dh],
                                   device(x + dx, y, h * 4 + zl, c)))
    own = kbuf[zh]
    for copy in shares:
        copy.wait_recv()
    for k in range(1, 8):
        own = own + krx[k]
    own = own[0:2]
    result = own[:, 0:32]
    for k in range(1, 4):
        result = jnp.where(x == k, own[:, 32 * k:32 * k + 32], result)
    out[...] = result
    for copy in sends:
        copy.wait_send()


def local(strain, green, weights, mask):
    return pl.pallas_call(
        kernel,
        out_shape=jax.ShapeDtypeStruct((2, 32), jnp.float32),
        in_specs=[
            pl.BlockSpec(memory_space=pl.ANY),
            pl.BlockSpec(memory_space=pl.ANY),
            pl.BlockSpec(memory_space=pltpu.VMEM),
            pl.BlockSpec(memory_space=pltpu.VMEM),
        ],
        out_specs=pl.BlockSpec(memory_space=pltpu.VMEM),
        scratch_shapes=[
            pltpu.VMEM((2, 4, 4, 12, 16, 256), jnp.bfloat16),
            pltpu.VMEM((2, 4, 4, 6, 16, 128), jnp.bfloat16),
            pltpu.VMEM((6, 768, 256), jnp.bfloat16),
            pltpu.VMEM((1024, 768), jnp.bfloat16),
            pltpu.VMEM((6, 1024, 256), jnp.float32),
            pltpu.VMEM((2, 16, 256), jnp.float32),
            pltpu.VMEM((2, 8, 128), jnp.float32),
            pltpu.VMEM((8, 8, 128), jnp.float32),
            pltpu.SemaphoreType.DMA((7,)),
            pltpu.SemaphoreType.DMA((64,)),
            pltpu.SemaphoreType.DMA((2, 4, 4)),
            pltpu.SemaphoreType.DMA((3, 6)),
            pltpu.SemaphoreType.DMA((4,)),
            pltpu.SemaphoreType.DMA((4,)),
            pltpu.SemaphoreType.DMA((1,)),
            pltpu.SemaphoreType.DMA((8,)),
        ],
        compiler_params=pltpu.CompilerParams(
            collective_id=0, has_side_effects=True, vmem_limit_bytes=60 << 20),
    )(strain.reshape(12, *strain.shape[2:]), jnp.swapaxes(green, 2, 3).reshape(6, 6, 128, 256),
      weights.reshape(6, *weights.shape[2:]), mask)


def solution(mesh):
    return jax.shard_map(
        local,
        mesh=mesh,
        in_specs=(
            P(None, None, "ev", None),
            P(None, None, "st", None, "ev"),
            P(None, None, "ev", "st"),
            P("ev", "st"),
        ),
        out_specs=P(None, ("ev", "st")),
        check_vma=False,
    )
```

time: 154 us -> 50.3 us (0.33)
  waiting for transfers between devices: 70.7 us -> 0 us
  Pallas kernels: 0 us -> 48.9 us
  local copies, waits for them, and re-layouts: 33.1 us -> 1.24 us
  starting transfers between devices: 19.3 us -> 0 us
  blocking collectives: 16.7 us -> 0 us
  other arithmetic: 9.18 us -> 0 us
  matrix products: 3.47 us -> 0 us
    all_to_all x3 -> x0, waiting for transfers between devices: 70.7 us -> none  [the longest x2 50.5 us: turned_blocks(): lax.all_to_all(blocks, axes[k], split_axis=k, concat_axis=k, tiled=True)]
    pallas_call x0 -> x1, Pallas kernels: none -> 48.9 us  [local(): pl.pallas_call(kernel, out_shape=jax.ShapeDtypeStruct((2, 32), jnp.float3...]
    all_to_all x3 -> x0, starting transfers between devices: 19.3 us -> none  [the longest x2 12 us: turned_blocks(): lax.all_to_all(blocks, axes[k], split_axis=k, concat_axis=k, tiled=True)]
    all_to_all x1 -> x0, blocking collectives: 16.7 us -> none  [sent_and_summed(): blocks = lax.all_to_all(in_blocks(x, dim, count), axis, 0, 0, tiled=True)]
    sub x2 -> x0, local copies, waits for them, and re-layouts: 7.06 us -> none  [local(): products[0, 0] - products[1, 1]]
    unnamed x12 -> x1, local copies, waits for them, and re-layouts: 7.92 us -> 1.24 us
    reduce_sum x6 -> x0, other arithmetic: 5.1 us -> none  [the longest x1 1.62 us: local(): held_real[:, :3].sum(1)]
    add x2 -> x0, local copies, waits for them, and re-layouts: 4.79 us -> none  [local(): products[0, 1] + products[1, 0]]
  transfers between devices with their start and end apart: 3 -> 0, of which waited for: 3 -> 0; matrix products, arithmetic and copies ran while one was open for 20% -> 0% of each run, Pallas kernels for 0% -> 0%
where the time goes in v1:
time: 50.3 us; the launch traced here: 50.2 us
  Pallas kernels  48.9 us (97%)
  local copies, waits for them, and re-layouts  1.24 us (2%)
    pallas_call x1, Pallas kernels, local(): pl.pallas_call(kernel, out_shape=jax.ShapeDtypeStruct((2, 32), jnp.float3...  48.9 us
    unnamed x1, local copies, waits for them, and re-layouts  1.24 us

profile of v1, /device:TPU:1, one launch (start us, length us, event | category | flops | bytes accessed | tf_op | source)
XLA Modules:
  0.0 50.2 jit_solution(6475790047891938837)
XLA Ops:
  0.0 48.9 %shard_map.46 = f32[2,32]{1,0:T(2,128)} custom-call(bf16[12,16,8192]{2,1,0:T(8,128)(2,1)} %bitcast.5, bf16[6,6,128,256]{3,2,1,0:T(8,128)(2,1)} %bitcast.6, bf16[6,16,128]{2,1,0:T(8,128)(2,1)} %bitcast.7, s32[16,128]{1,0:T(8,128)} %mask.1), custom_call_target="tpu_custom_call" | custom-call | tf_op jit(solution)/shard_map/pallas_call | solution.py:199
  49.0 1.2 %copy.6 = f32[2,32]{1,0:T(2,128)} copy(f32[2,32]{1,0:T(2,128)} %shard_map.46) | data formatting | bytes 512

commit v2 on v1

--- a/solution.py
+++ b/solution.py
@@ -6,8 +6,8 @@
 from jax.sharding import PartitionSpec as P
 
 MESH = pl.DeviceIdType.MESH
-OFF_AXIS = (1, 3, 2)
-GROUPS = tuple((dc, dy) for dy in OFF_AXIS for dc in (0, 1))
+CORNERS = ((1, 1), (3, 3), (1, 3), (3, 1), (1, 2), (2, 1), (3, 2), (2, 3), (2, 2))
+ALONG = ((1, 0), (0, 1), (3, 0), (0, 3), (2, 0), (0, 2))
 
 
 def kernel(strain, green, weights, mask, out, sbuf, wbuf, gs, lhs, held, acc, kbuf, krx,
@@ -50,17 +50,15 @@
 
     barrier = pltpu.get_barrier_semaphore()
     senders = [device(x, y, z, 1 - c)]
-    for dy in range(4):
-        for dz in range(4):
+    for dy in (2, 1, 3, 0):
+        for dz in (2, 1, 3, 0):
             if dy or dz:
                 for core in (0, 1):
                     senders.append(device(x, y - dy, z - far(dz, c), core))
     for dz in (1, 2, 3):
         senders.append(device(x, y, in_half(4 - dz), c))
-    for dx in range(4):
-        for dh in (0, 4):
-            if dx or dh:
-                senders.append(device(x + dx, y, z + dh, c))
+    for dx in (1, 3):
+        senders.append(device(x + dx, y, z, c))
     for d in senders:
         pl.semaphore_signal(barrier, inc=1, device_id=d, device_id_type=MESH)
     wbuf[0, 0, 0] = weights[...] * mask[...].astype(jnp.bfloat16)[None]
@@ -74,71 +72,90 @@
         to = device(x, y + dy, z + far(dz, core), core)
         return send(strain.at[slabs, :, cells(to[0])], sbuf.at[dc, dy, dz, slabs], r_s.at[dc, dy, dz], to)
 
-    quarters = {}
-    for dc, dy in GROUPS:
-        quarters[dc, dy] = [strain_to(dy, dz, dc, mine) for dz in (1, 2, 3)]
+    corner = {}
+    for dy, dz in CORNERS:
+        corner[dy, dz] = [strain_to(dy, dz, dc, mine) for dc in (0, 1)]
     whole = pl.ds(0, 12)
-    direct = [strain_to(0, 0, 1, whole)]
-    for dy, dz in ((1, 0), (0, 1), (3, 0), (0, 3), (2, 0), (0, 2)):
-        for dc in (0, 1):
-            direct.append(strain_to(dy, dz, dc, whole))
 
     for copy in wz:
         copy.wait_recv()
     wy = [send(wbuf.at[0, 0], wbuf.at[0, dy], r_wy.at[dy], device(x, y + dy, z, c)) for dy in (1, 3, 2)]
+    direct = [strain_to(dy, dz, dc, whole) for dy, dz in ALONG for dc in (0, 1)]
+    direct.append(strain_to(0, 0, 1, whole))
 
     right, left = device(x + 1, y, z, c), device(x - 1, y, z, c)
 
-    def part(dc, dy, of_x):
-        return sbuf.at[dc, dy, pl.ds(1, 3), pl.ds(3 * ((of_x + 4) % 4), 3)]
-
-    to_right, to_left, relays = {}, {}, {}
-    for g, (dc, dy) in enumerate(GROUPS):
-        for copy in quarters[dc, dy]:
+    def part(dcs, g, of_x):
+        return sbuf.at[dcs, CORNERS[g][0], CORNERS[g][1], pl.ds(3 * ((of_x + 4) % 4), 3)]
+
+    to_right, to_left, relay_right, relay_left = {}, {}, {}, {}
+    both = pl.ds(0, 2)
+
+    def forward(g):
+        for copy in corner[CORNERS[g]]:
             copy.wait_recv()
-        p = part(dc, dy, x)
+        p = part(both, g, x)
         to_right[g] = send(p, p, r_x.at[0, g], right)
         to_left[g] = send(p, p, r_x.at[1, g], left)
 
-    for copy in wy:
-        copy.wait_recv()
-    wc = send(wbuf.at[0], wbuf.at[1], r_wc.at[0], device(x, y, z, 1 - c))
-
     def relay(g):
-        dc, dy = GROUPS[g]
-        if dc == 0:
-            to_right[g].wait_recv()
-            p = part(dc, dy, x - 1)
-            relays[g] = send(p, p, r_x.at[2, g], right)
-        else:
-            to_left[g].wait_recv()
-            p = part(dc, dy, x + 1)
-            relays[g] = send(p, p, r_x.at[2, g], left)
-
-    relay(0)
-    relay(1)
-    wc.wait_recv()
-    all_w = wbuf.reshape(32, 6, 16, 128)
-    for f in range(3):
-        real = all_w[:, f].reshape(512, 128)
-        imag = all_w[:, 3 + f].reshape(512, 128)
-        lhs[0:512, f * 128:(f + 1) * 128] = real
-        lhs[0:512, 384 + f * 128:384 + (f + 1) * 128] = -imag
-        lhs[512:1024, f * 128:(f + 1) * 128] = imag
-        lhs[512:1024, 384 + f * 128:384 + (f + 1) * 128] = real
+        to_right[g].wait_recv()
+        p = part(0, g, x - 1)
+        relay_right[g] = send(p, p, r_x.at[2, g], right)
+        to_left[g].wait_recv()
+        p = part(1, g, x + 1)
+        relay_left[g] = send(p, p, r_x.at[3, g], left)
+
+    def middle_weights():
+        for copy in wy:
+            copy.wait_recv()
+        sib.append(send(wbuf.at[0], wbuf.at[1], r_wc.at[0], device(x, y, z, 1 - c)))
+
+    sib = []
+
+    def left_side():
+        sib[0].wait_recv()
+        all_w = wbuf.reshape(32, 6, 16, 128)
+        for f in range(3):
+            real = all_w[:, f].reshape(512, 128)
+            imag = all_w[:, 3 + f].reshape(512, 128)
+            lhs[0:512, f * 128:(f + 1) * 128] = real
+            lhs[0:512, 384 + f * 128:384 + (f + 1) * 128] = -imag
+            lhs[512:1024, f * 128:(f + 1) * 128] = imag
+            lhs[512:1024, 384 + f * 128:384 + (f + 1) * 128] = real
+        for copy in load_green:
+            copy.wait()
 
     def multiply(v, _):
         held[v] = jnp.dot(lhs[...], gs[v], preferred_element_type=jnp.float32)
         return 0
 
-    for copy in load_green:
-        copy.wait()
-    lax.fori_loop(0, 3, multiply, 0)
+    def products(first, last):
+        lax.fori_loop(first, last, multiply, 0)
+
+    forward(0)
+    forward(1)
+    forward(2)
+    forward(3)
+    relay(0)
+    relay(1)
+    forward(4)
+    forward(5)
     relay(2)
     relay(3)
-    lax.fori_loop(3, 6, multiply, 0)
+    forward(6)
+    forward(7)
     relay(4)
     relay(5)
+    middle_weights()
+    forward(8)
+    relay(6)
+    left_side()
+    products(0, 2)
+    relay(7)
+    products(2, 4)
+    relay(8)
+    products(4, 6)
 
     acc[...] = jnp.zeros_like(acc)
 
@@ -159,16 +176,16 @@
     for copy in direct:
         copy.wait_recv()
     add_up((1, 0, 0))
-    for dy, dz in ((1, 0), (0, 1), (3, 0), (0, 3), (2, 0), (0, 2)):
+    for dy, dz in ALONG:
         for dc in (0, 1):
             add_up((dc, dy, dz))
-    for g, (dc, dy) in enumerate(GROUPS):
-        if dc == 0:
-            to_left[g].wait_recv()
-        else:
-            to_right[g].wait_recv()
-        relays[g].wait_recv()
-        for dz in (1, 2, 3):
+    for copy in sends:
+        copy.wait_send()
+    done = len(sends)
+    for g, (dy, dz) in enumerate(CORNERS):
+        relay_right[g].wait_recv()
+        relay_left[g].wait_recv()
+        for dc in (0, 1):
             add_up((dc, dy, dz))
 
     total = acc[...].sum(axis=1)
@@ -191,7 +208,7 @@
     for k in range(1, 4):
         result = jnp.where(x == k, own[:, 32 * k:32 * k + 32], result)
     out[...] = result
-    for copy in sends:
+    for copy in sends[done:]:
         copy.wait_send()
 
 
@@ -216,9 +233,9 @@
             pltpu.VMEM((2, 8, 128), jnp.float32),
             pltpu.VMEM((8, 8, 128), jnp.float32),
             pltpu.SemaphoreType.DMA((7,)),
-            pltpu.SemaphoreType.DMA((64,)),
+            pltpu.SemaphoreType.DMA((88,)),
             pltpu.SemaphoreType.DMA((2, 4, 4)),
-            pltpu.SemaphoreType.DMA((3, 6)),
+            pltpu.SemaphoreType.DMA((4, 9)),
             pltpu.SemaphoreType.DMA((4,)),
             pltpu.SemaphoreType.DMA((4,)),
             pltpu.SemaphoreType.DMA((1,)),

time: 50.3 us -> 44.2 us (0.88)
  Pallas kernels: 48.9 us -> 42.8 us
    pallas_call x1, Pallas kernels: 48.9 us -> 42.8 us  [local(): pl.pallas_call(kernel, out_shape=jax.ShapeDtypeStruct((2, 32), jnp.float3...]
where the time goes in v2:
time: 44.2 us; the launch traced here: 44.1 us
  Pallas kernels  42.8 us (97%)
  local copies, waits for them, and re-layouts  1.24 us (3%)
    pallas_call x1, Pallas kernels, local(): pl.pallas_call(kernel, out_shape=jax.ShapeDtypeStruct((2, 32), jnp.float3...  42.8 us
    unnamed x1, local copies, waits for them, and re-layouts  1.24 us

profile of v2, /device:TPU:1, one launch (start us, length us, event | category | flops | bytes accessed | tf_op | source)
XLA Modules:
  0.0 44.1 jit_solution(5696278749428649900)
XLA Ops:
  0.0 42.8 %shard_map.46 = f32[2,32]{1,0:T(2,128)} custom-call(bf16[12,16,8192]{2,1,0:T(8,128)(2,1)} %bitcast.5, bf16[6,6,128,256]{3,2,1,0:T(8,128)(2,1)} %bitcast.6, bf16[6,16,128]{2,1,0:T(8,128)(2,1)} %bitcast.7, s32[16,128]{1,0:T(8,128)} %mask.1), custom_call_target="tpu_custom_call" | custom-call | tf_op jit(solution)/shard_map/pallas_call | solution.py:216
  42.9 1.2 %copy.6 = f32[2,32]{1,0:T(2,128)} copy(f32[2,32]{1,0:T(2,128)} %shard_map.46) | data formatting | bytes 512

commit v3 on v0

v3 whole, which is shorter than its diff:
```python
import jax
import jax.numpy as jnp
from jax import lax
from jax.experimental import pallas as pl
from jax.experimental.pallas import tpu as pltpu
from jax.sharding import PartitionSpec as P

MESH = pl.DeviceIdType.MESH
CORNERS = ((1, 1), (3, 3), (1, 3), (3, 1), (1, 2), (3, 2), (2, 1), (2, 3), (2, 2))
ALONG = ((1, 0), (0, 1), (3, 0), (0, 3), (2, 0), (0, 2))
FAR, NEAR, WHOLE = 0, 1, 2
WHOLE_GROUPS, WHOLE_ALONG = 6, 4


def kernel(strain, green, weights, mask, out, sbuf, wbuf, gs, lhs, held, acc, kbuf, krx,
           lsem, s_all, r_w, r_c, r_d, r_f, r_r, r_k):
    ev, st = lax.axis_index("ev"), lax.axis_index("st")
    y, zl, c = ev >> 3, (ev >> 1) & 3, ev & 1
    zh, x = st >> 2, st & 3
    z = zh * 4 + zl
    cores = (c, 1 - c)
    row = [((y + dy) & 3) * 8 for dy in range(4)]
    step_z = {(0, k): 0 for k in (0, 1)} | {(1, k): 1 for k in (0, 1)} | {(3, k): -1 for k in (0, 1)}
    step_z |= {(2, k): 2 - 4 * cores[k] for k in (0, 1)}
    place_to = {at: (z + step) & 7 for at, step in step_z.items()}
    place_from = {dz: (z - step_z[dz, 0]) & 7 for dz in range(4)}
    place_half = [zh * 4 + ((zl + dz) & 3) for dz in range(4)]
    xs = [(x + dx) & 3 for dx in range(4)]

    def device(x_, row_, place, core):
        return (row_ + (place & 3) * 2 + core, (place >> 2) * 4 + x_)

    def lanes(part, half):
        if part == WHOLE:
            return pl.ds(0, 256)
        return pl.ds(pl.multiple_of((1 - half if part == FAR else half) * 128, 128), 128)

    def send(src, dst, send_sem, recv_sem, to):
        pltpu.make_async_remote_copy(
            src_ref=src, dst_ref=dst, send_sem=send_sem, recv_sem=recv_sem,
            device_id=to, device_id_type=MESH).start()

    def arrived(ref, sem):
        pltpu.make_async_remote_copy(
            src_ref=ref, dst_ref=ref, send_sem=s_all.at[0], recv_sem=sem,
            device_id=right, device_id_type=MESH).wait_recv()

    def left(ref, sem):
        pltpu.make_async_remote_copy(
            src_ref=ref, dst_ref=ref, send_sem=sem, recv_sem=r_w.at[0],
            device_id=right, device_id_type=MESH).wait_send()

    right_of, left_of = (ev, zh * 4 + xs[1]), (ev, zh * 4 + xs[3])
    right = right_of
    across = (ev + 1 - 2 * c, st)

    barrier = pltpu.get_barrier_semaphore()
    senders = []
    for dy in (2, 1, 3, 0):
        for dz in (2, 1, 3, 0):
            if dy or dz:
                for core in (0, 1):
                    senders.append(device(x, row[-dy], place_from[dz], core))
    for dz in (1, 2, 3):
        senders.append(device(x, row[0], place_half[4 - dz], c))
    for dx in (1, 3):
        senders.append((ev, zh * 4 + xs[dx]))
    senders.append((ev + 1 - 2 * c, st))
    for d in senders:
        pl.semaphore_signal(barrier, inc=1, device_id=d, device_id_type=MESH)

    load_green = [
        pltpu.make_async_copy(green.at[k], gs.at[:, pl.ds(k * 128, 128), :], lsem.at[1 + k]) for k in range(6)]
    for copy in load_green:
        copy.start()
    own_cells = pl.ds(pl.multiple_of(ev * 256, 256), 256)
    load_own = pltpu.make_async_copy(strain.at[:, :, own_cells], sbuf.at[0, 0, 0], lsem.at[0])
    load_own.start()
    wbuf[0, 0, 0] = weights[...] * mask[...].astype(jnp.bfloat16)[None]
    pl.semaphore_wait(barrier, len(senders))

    for dz in (1, 2, 3):
        send(wbuf.at[0, 0, 0], wbuf.at[0, 0, dz], s_all.at[0], r_w.at[0], device(x, row[0], place_half[dz], c))

    mine = pl.ds(3 * x, 3)
    whole = pl.ds(0, 12)
    both = pl.ds(0, 2)

    def strain_to(dy, dz, dc, slabs, part, send_sem, recv_sem):
        place = place_to[dz, dc]
        to = device(x, row[dy], place, cores[dc])
        at = lanes(part, place >> 2)
        start = pl.multiple_of(to[0] * 256 + at.start, 128)
        send(strain.at[slabs, :, pl.ds(start, at.size)], sbuf.at[dc, dy, dz, slabs, :, at], send_sem, recv_sem, to)

    def parts_of(count, first_split):
        for n in range(first_split):
            yield n, WHOLE
        for part in (FAR, NEAR):
            for n in range(first_split, count):
                yield n, part

    GP = list(parts_of(9, WHOLE_GROUPS))
    DP = list(parts_of(6, WHOLE_ALONG))

    def send_corner(g, part):
        for dc in (0, 1):
            strain_to(*CORNERS[g], dc, mine, part, s_all.at[3], r_c.at[g, part])

    def send_direct(n, part):
        for dc in (0, 1):
            strain_to(*ALONG[n], dc, whole, part, s_all.at[4], r_d.at[n, part])

    strain_to(0, 0, 1, whole, WHOLE, s_all.at[5], r_w.at[3])
    for g, part in GP:
        send_corner(g, part)
    arrived(wbuf.at[0, 0, pl.ds(1, 3)], r_w.at[0])
    for dy in (1, 3, 2):
        send(wbuf.at[0, 0], wbuf.at[0, dy], s_all.at[1], r_w.at[1], (row[dy] + (ev & 7), st))
    for n, part in DP:
        send_direct(n, part)

    def block(dcs, g, slabs, part):
        return sbuf.at[dcs, CORNERS[g][0], CORNERS[g][1], slabs, :, lanes(part, zh)]

    def forward(g, part):
        b = block(both, g, mine, part)
        arrived(b, r_c.at[g, part])
        for to in (right_of, left_of):
            send(b, b, s_all.at[6], r_f.at[g, part], to)

    def relay(g, part):
        arrived(block(both, g, pl.ds(0, 6), part), r_f.at[g, part])
        for dc, of_x, to in ((0, xs[3], right_of), (1, xs[1], left_of)):
            b = block(dc, g, pl.ds(3 * of_x, 3), part)
            send(b, b, s_all.at[7], r_r.at[g, part], to)

    def weights_across():
        arrived(wbuf.at[0, pl.ds(1, 3)], r_w.at[1])
        send(wbuf.at[0], wbuf.at[1], s_all.at[2], r_w.at[2], across)

    def left_side():
        arrived(wbuf.at[1], r_w.at[2])
        all_w = wbuf.reshape(32, 6, 16, 128)
        for f in range(3):
            real = all_w[:, f].reshape(512, 128)
            imag = all_w[:, 3 + f].reshape(512, 128)
            lhs[0:512, f * 128:(f + 1) * 128] = real
            lhs[0:512, 384 + f * 128:384 + (f + 1) * 128] = -imag
            lhs[512:1024, f * 128:(f + 1) * 128] = imag
            lhs[512:1024, 384 + f * 128:384 + (f + 1) * 128] = real
        for copy in load_green:
            copy.wait()

    def multiply(v, _):
        held[v] = jnp.dot(lhs[...], gs[v], preferred_element_type=jnp.float32)
        return 0

    def products(first, last):
        lax.fori_loop(first, last, multiply, 0)

    acc[...] = jnp.zeros_like(acc)

    def add_up(slot, part):
        dc, dy, dz = slot
        first = (dc * 16 + dy * 4 + dz) * 16
        at = lanes(part, zh)
        s = sbuf[dc, dy, dz, :, :, at].astype(jnp.float32)
        hr = [held[v, pl.ds(first, 16), at] for v in range(6)]
        hi = [held[v, pl.ds(512 + first, 16), at] for v in range(6)]
        trace = (s[0] + s[1] + s[2]) * (hr[0] + hr[1] + hr[2]) - (s[6] + s[7] + s[8]) * (hi[0] + hi[1] + hi[2])
        normal = sum(s[v] * hr[v] - s[6 + v] * hi[v] for v in range(3))
        shear = sum(s[v] * hr[v] - s[6 + v] * hi[v] for v in range(3, 6))
        acc[0, :, at] += trace
        acc[1, :, at] += normal + 2.0 * shear

    def take_direct(n, part):
        arrived(sbuf.at[both, ALONG[n][0], ALONG[n][1], :, :, lanes(part, zh)], r_d.at[n, part])
        for dc in (0, 1):
            add_up((dc, *ALONG[n]), part)

    def take_corner(g, part):
        arrived(block(both, g, pl.ds(0, 3), part), r_r.at[g, part])
        for dc in (0, 1):
            add_up((dc, *CORNERS[g]), part)

    def share(dh):
        kbuf[dh, 0:2] = acc[:, :, lanes(NEAR if dh == 0 else FAR, zh)].sum(axis=1)
        for dx in (2, 1, 3, 0):
            if dx or dh:
                send(kbuf.at[dh], krx.at[4 * dh + dx], s_all.at[8 + dh], r_k.at[dh], (ev, (zh ^ dh) * 4 + xs[dx]))

    for stage in GP[0:6]:
        forward(*stage)
    for stage in GP[0:2]:
        relay(*stage)
    for stage in GP[6:9]:
        forward(*stage)
    for stage in GP[2:4]:
        relay(*stage)
    for stage in GP[9:12]:
        forward(*stage)
    relay(*GP[4])
    weights_across()
    for stage in GP[5:8]:
        relay(*stage)
    left_side()
    products(0, 3)
    relay(*GP[8])
    products(3, 6)
    for stage in GP[9:12]:
        relay(*stage)
    load_own.wait()
    add_up((0, 0, 0), WHOLE)
    arrived(sbuf.at[1, 0, 0], r_w.at[3])
    add_up((1, 0, 0), WHOLE)
    for stage in DP[0:4]:
        take_direct(*stage)
    for stage in GP[0:6]:
        take_corner(*stage)
    for stage in DP[4:6]:
        take_direct(*stage)
    for stage in GP[6:9]:
        take_corner(*stage)
    share(1)
    for stage in DP[6:8]:
        take_direct(*stage)
    for stage in GP[9:12]:
        take_corner(*stage)
    share(0)
    left(wbuf.at[0, 0, pl.ds(1, 3)], s_all.at[0])
    left(wbuf.at[0, pl.ds(1, 3)], s_all.at[1])
    left(wbuf.at[0], s_all.at[2])
    left(sbuf.at[0, pl.ds(0, 3), pl.ds(0, 3), pl.ds(0, 6)], s_all.at[3])
    left(sbuf.at[0, pl.ds(0, 3)], s_all.at[4])
    left(sbuf.at[0, 0, 0], s_all.at[5])
    left(sbuf.at[0, pl.ds(0, 3), pl.ds(0, 3)], s_all.at[6])
    left(sbuf.at[0, pl.ds(0, 3), pl.ds(0, 3), pl.ds(0, 6)], s_all.at[7])
    arrived(krx.at[pl.ds(4, 4)], r_k.at[1])
    other = krx[4] + krx[5] + krx[6] + krx[7]
    arrived(krx.at[pl.ds(1, 3)], r_k.at[0])
    same = kbuf[0] + krx[1] + krx[2] + krx[3]

    def own_cells_of(total):
        result = total[0:2, 0:32]
        for k in range(1, 4):
            result = jnp.where(x == k, total[0:2, 32 * k:32 * k + 32], result)
        return result

    out[0] = own_cells_of(same)
    out[1] = own_cells_of(other)
    left(krx.at[pl.ds(1, 3)], s_all.at[8])
    left(krx.at[pl.ds(4, 4)], s_all.at[9])


def local(strain, green, weights, mask):
    sums = pl.pallas_call(
        kernel,
        out_shape=jax.ShapeDtypeStruct((2, 2, 32), jnp.float32),
        in_specs=[
            pl.BlockSpec(memory_space=pl.ANY),
            pl.BlockSpec(memory_space=pl.ANY),
            pl.BlockSpec(memory_space=pltpu.VMEM),
            pl.BlockSpec(memory_space=pltpu.VMEM),
        ],
        out_specs=pl.BlockSpec(memory_space=pltpu.VMEM),
        scratch_shapes=[
            pltpu.VMEM((2, 4, 4, 12, 16, 256), jnp.bfloat16),
            pltpu.VMEM((2, 4, 4, 6, 16, 128), jnp.bfloat16),
            pltpu.VMEM((6, 768, 256), jnp.bfloat16),
            pltpu.VMEM((1024, 768), jnp.bfloat16),
            pltpu.VMEM((6, 1024, 256), jnp.float32),
            pltpu.VMEM((2, 16, 256), jnp.float32),
            pltpu.VMEM((2, 8, 128), jnp.float32),
            pltpu.VMEM((8, 8, 128), jnp.float32),
            pltpu.SemaphoreType.DMA((7,)),
            pltpu.SemaphoreType.DMA((10,)),
            pltpu.SemaphoreType.DMA((4,)),
            pltpu.SemaphoreType.DMA((9, 3)),
            pltpu.SemaphoreType.DMA((6, 3)),
            pltpu.SemaphoreType.DMA((9, 3)),
            pltpu.SemaphoreType.DMA((9, 3)),
            pltpu.SemaphoreType.DMA((2,)),
        ],
        compiler_params=pltpu.CompilerParams(
            collective_id=0, has_side_effects=True, vmem_limit_bytes=60 << 20),
    )(strain.reshape(12, *strain.shape[2:]), jnp.swapaxes(green, 2, 3).reshape(6, 6, 128, 256),
      weights.reshape(6, *weights.shape[2:]), mask)
    return sums[0] + sums[1]


def solution(mesh):
    return jax.shard_map(
        local,
        mesh=mesh,
        in_specs=(
            P(None, None, "ev", None),
            P(None, None, "st", None, "ev"),
            P(None, None, "ev", "st"),
            P("ev", "st"),
        ),
        out_specs=P(None, ("ev", "st")),
        check_vma=False,
    )
```

time: 154 us -> 41.2 us (0.27)
  waiting for transfers between devices: 70.7 us -> 0 us
  Pallas kernels: 0 us -> 39.7 us
  local copies, waits for them, and re-layouts: 33.1 us -> 0 us
  starting transfers between devices: 19.3 us -> 0 us
  blocking collectives: 16.7 us -> 0 us
  other arithmetic: 9.18 us -> 1.25 us
  matrix products: 3.47 us -> 0 us
    all_to_all x3 -> x0, waiting for transfers between devices: 70.7 us -> none  [the longest x2 50.5 us: turned_blocks(): lax.all_to_all(blocks, axes[k], split_axis=k, concat_axis=k, tiled=True)]
    pallas_call x0 -> x1, Pallas kernels: none -> 39.7 us  [local(): pl.pallas_call(kernel, out_shape=jax.ShapeDtypeStruct((2, 2, 32), jnp.flo...]
    all_to_all x3 -> x0, starting transfers between devices: 19.3 us -> none  [the longest x2 12 us: turned_blocks(): lax.all_to_all(blocks, axes[k], split_axis=k, concat_axis=k, tiled=True)]
    all_to_all x1 -> x0, blocking collectives: 16.7 us -> none  [sent_and_summed(): blocks = lax.all_to_all(in_blocks(x, dim, count), axis, 0, 0, tiled=True)]
    unnamed x12 -> x0, local copies, waits for them, and re-layouts: 7.92 us -> none
    sub x2 -> x0, local copies, waits for them, and re-layouts: 7.06 us -> none  [local(): products[0, 0] - products[1, 1]]
    reduce_sum x6 -> x0, other arithmetic: 5.1 us -> none  [the longest x1 1.62 us: local(): held_real[:, :3].sum(1)]
    add x2 -> x0, local copies, waits for them, and re-layouts: 4.79 us -> none  [local(): products[0, 1] + products[1, 0]]
  transfers between devices with their start and end apart: 3 -> 0, of which waited for: 3 -> 0; matrix products, arithmetic and copies ran while one was open for 20% -> 0% of each run, Pallas kernels for 0% -> 0%
where the time goes in v3:
time: 41.2 us; the launch traced here: 40.9 us
  Pallas kernels  39.7 us (96%)
  other arithmetic  1.25 us (3%)
    pallas_call x1, Pallas kernels, local(): pl.pallas_call(kernel, out_shape=jax.ShapeDtypeStruct((2, 2, 32), jnp.flo...  39.7 us
    add x1, other arithmetic, local(): return sums[0] + sums[1]  1.25 us

profile of v3, /device:TPU:1, one launch (start us, length us, event | category | flops | bytes accessed | tf_op | source)
XLA Modules:
  0.0 40.9 jit_solution(6715232001788786231)
XLA Ops:
  0.0 39.7 %shard_map.46 = f32[2,2,32]{2,1,0:T(2,128)} custom-call(bf16[12,16,8192]{2,1,0:T(8,128)(2,1)} %bitcast.7, bf16[6,6,128,256]{3,2,1,0:T(8,128)(2,1)} %bitcast.8, bf16[6,16,128]{2,1,0:T(8,128)(2,1)} %bitcast.9, s32[16,128]{1,0:T(8,128)} %mask.1), custom_call_target="tpu_custom_call" | custom-call | tf_op jit(solution)/shard_map/pallas_call | solution.py:257
  39.7 1.3 %add_bitcast_fusion = f32[2,32]{1,0:T(2,128)} fusion(f32[2,2,32]{2,1,0:T(2,128)} %shard_map.46), kind=kLoop, calls=%fused_computation | loop fusion | flops 64 | bytes 768 | tf_op jit(solution)/shard_map/add | solution.py:289

commit v4 on v3

--- a/solution.py
+++ b/solution.py
@@ -12,7 +12,7 @@
 WHOLE_GROUPS, WHOLE_ALONG = 6, 4
 
 
-def kernel(strain, green, weights, mask, out, sbuf, wbuf, gs, lhs, held, acc, kbuf, krx,
+def kernel(strain, green, weights, mask, out, sbuf, wbuf, gs, lhs, held, acc, kbuf, krx, wraw, mraw,
            lsem, s_all, r_w, r_c, r_d, r_f, r_r, r_k):
     ev, st = lax.axis_index("ev"), lax.axis_index("st")
     y, zl, c = ev >> 3, (ev >> 1) & 3, ev & 1
@@ -69,6 +69,10 @@
     for d in senders:
         pl.semaphore_signal(barrier, inc=1, device_id=d, device_id_type=MESH)
 
+    load_pair = [
+        pltpu.make_async_copy(weights, wraw, lsem.at[7]), pltpu.make_async_copy(mask, mraw, lsem.at[8])]
+    for copy in load_pair:
+        copy.start()
     load_green = [
         pltpu.make_async_copy(green.at[k], gs.at[:, pl.ds(k * 128, 128), :], lsem.at[1 + k]) for k in range(6)]
     for copy in load_green:
@@ -76,7 +80,9 @@
     own_cells = pl.ds(pl.multiple_of(ev * 256, 256), 256)
     load_own = pltpu.make_async_copy(strain.at[:, :, own_cells], sbuf.at[0, 0, 0], lsem.at[0])
     load_own.start()
-    wbuf[0, 0, 0] = weights[...] * mask[...].astype(jnp.bfloat16)[None]
+    for copy in load_pair:
+        copy.wait()
+    wbuf[0, 0, 0] = wraw[...] * mraw[...].astype(jnp.bfloat16)[None]
     pl.semaphore_wait(barrier, len(senders))
 
     for dz in (1, 2, 3):
@@ -112,13 +118,10 @@
             strain_to(*ALONG[n], dc, whole, part, s_all.at[4], r_d.at[n, part])
 
     strain_to(0, 0, 1, whole, WHOLE, s_all.at[5], r_w.at[3])
-    for g, part in GP:
-        send_corner(g, part)
-    arrived(wbuf.at[0, 0, pl.ds(1, 3)], r_w.at[0])
-    for dy in (1, 3, 2):
-        send(wbuf.at[0, 0], wbuf.at[0, dy], s_all.at[1], r_w.at[1], (row[dy] + (ev & 7), st))
-    for n, part in DP:
-        send_direct(n, part)
+    def weights_up():
+        arrived(wbuf.at[0, 0, pl.ds(1, 3)], r_w.at[0])
+        for dy in (1, 3, 2):
+            send(wbuf.at[0, 0], wbuf.at[0, dy], s_all.at[1], r_w.at[1], (row[dy] + (ev & 7), st))
 
     def block(dcs, g, slabs, part):
         return sbuf.at[dcs, CORNERS[g][0], CORNERS[g][1], slabs, :, lanes(part, zh)]
@@ -190,17 +193,15 @@
             if dx or dh:
                 send(kbuf.at[dh], krx.at[4 * dh + dx], s_all.at[8 + dh], r_k.at[dh], (ev, (zh ^ dh) * 4 + xs[dx]))
 
-    for stage in GP[0:6]:
+    for stage in GP[0:12]:
+        send_corner(*stage)
+    weights_up()
+    for stage in DP[0:8]:
+        send_direct(*stage)
+    for stage in GP[0:12]:
         forward(*stage)
-    for stage in GP[0:2]:
+    for stage in GP[0:5]:
         relay(*stage)
-    for stage in GP[6:9]:
-        forward(*stage)
-    for stage in GP[2:4]:
-        relay(*stage)
-    for stage in GP[9:12]:
-        forward(*stage)
-    relay(*GP[4])
     weights_across()
     for stage in GP[5:8]:
         relay(*stage)
@@ -208,14 +209,14 @@
     products(0, 3)
     relay(*GP[8])
     products(3, 6)
-    for stage in GP[9:12]:
-        relay(*stage)
     load_own.wait()
     add_up((0, 0, 0), WHOLE)
     arrived(sbuf.at[1, 0, 0], r_w.at[3])
     add_up((1, 0, 0), WHOLE)
     for stage in DP[0:4]:
         take_direct(*stage)
+    for stage in GP[9:12]:
+        relay(*stage)
     for stage in GP[0:6]:
         take_corner(*stage)
     for stage in DP[4:6]:
@@ -256,12 +257,12 @@
 def local(strain, green, weights, mask):
     sums = pl.pallas_call(
         kernel,
-        out_shape=jax.ShapeDtypeStruct((2, 2, 32), jnp.float32),
+        out_shape=pltpu.VMEM((2, 2, 32), jnp.float32),
         in_specs=[
             pl.BlockSpec(memory_space=pl.ANY),
             pl.BlockSpec(memory_space=pl.ANY),
-            pl.BlockSpec(memory_space=pltpu.VMEM),
-            pl.BlockSpec(memory_space=pltpu.VMEM),
+            pl.BlockSpec(memory_space=pl.ANY),
+            pl.BlockSpec(memory_space=pl.ANY),
         ],
         out_specs=pl.BlockSpec(memory_space=pltpu.VMEM),
         scratch_shapes=[
@@ -273,7 +274,9 @@
             pltpu.VMEM((2, 16, 256), jnp.float32),
             pltpu.VMEM((2, 8, 128), jnp.float32),
             pltpu.VMEM((8, 8, 128), jnp.float32),
-            pltpu.SemaphoreType.DMA((7,)),
+            pltpu.VMEM((6, 16, 128), jnp.bfloat16),
+            pltpu.VMEM((16, 128), jnp.int32),
+            pltpu.SemaphoreType.DMA((9,)),
             pltpu.SemaphoreType.DMA((10,)),
             pltpu.SemaphoreType.DMA((4,)),
             pltpu.SemaphoreType.DMA((9, 3)),

time: 41.2 us -> 39.3 us (0.954)
  Pallas kernels: 39.7 us -> 38.6 us
  other arithmetic: 1.25 us -> 0.56 us
    pallas_call x1, Pallas kernels: 39.7 us -> 38.6 us  [local(): pl.pallas_call(kernel, out_shape=pltpu.VMEM((2, 2, 32), jnp.float32), in_...]
    add x1, other arithmetic: 1.25 us -> 0.56 us  [local(): return sums[0] + sums[1]]
where the time goes in v4:
time: 39.3 us; the launch traced here: 39.2 us
  Pallas kernels  38.6 us (98%)
  other arithmetic  0.56 us (1%)
    pallas_call x1, Pallas kernels, local(): pl.pallas_call(kernel, out_shape=pltpu.VMEM((2, 2, 32), jnp.float32), in_...  38.6 us

profile of v4, /device:TPU:1, one launch (start us, length us, event | category | flops | bytes accessed | tf_op | source)
XLA Modules:
  0.0 39.2 jit_solution(2488137897747906644)
XLA Ops:
  0.0 38.6 %shard_map.46 = f32[2,2,32]{2,1,0:T(2,128)S(1)} custom-call(bf16[12,16,8192]{2,1,0:T(8,128)(2,1)} %bitcast.7, bf16[6,6,128,256]{3,2,1,0:T(8,128)(2,1)} %bitcast.8, bf16[6,16,128]{2,1,0:T(8,128)(2,1)} %bitcast.9, s32[16,128]{1,0:T(8,128)} %mask.1), custom_call_target="tpu_custom_call" | custom-call | tf_op jit(solution)/shard_map/pallas_call | solution.py:258
  38.6 0.6 %add_bitcast_fusion = f32[2,32]{1,0:T(2,128)} fusion(f32[2,2,32]{2,1,0:T(2,128)S(1)} %shard_map.46), kind=kLoop, calls=%fused_computation | loop fusion | flops 64 | bytes 768 | tf_op jit(solution)/shard_map/add | solution.py:292

commit v5 on v4

--- a/solution.py
+++ b/solution.py
@@ -9,7 +9,7 @@
 CORNERS = ((1, 1), (3, 3), (1, 3), (3, 1), (1, 2), (3, 2), (2, 1), (2, 3), (2, 2))
 ALONG = ((1, 0), (0, 1), (3, 0), (0, 3), (2, 0), (0, 2))
 FAR, NEAR, WHOLE = 0, 1, 2
-WHOLE_GROUPS, WHOLE_ALONG = 6, 4
+WHOLE_GROUPS, WHOLE_ALONG = 6, 2
 
 
 def kernel(strain, green, weights, mask, out, sbuf, wbuf, gs, lhs, held, acc, kbuf, krx, wraw, mraw,
@@ -196,7 +196,7 @@
     for stage in GP[0:12]:
         send_corner(*stage)
     weights_up()
-    for stage in DP[0:8]:
+    for stage in DP[0:10]:
         send_direct(*stage)
     for stage in GP[0:12]:
         forward(*stage)
@@ -213,18 +213,18 @@
     add_up((0, 0, 0), WHOLE)
     arrived(sbuf.at[1, 0, 0], r_w.at[3])
     add_up((1, 0, 0), WHOLE)
-    for stage in DP[0:4]:
+    for stage in DP[0:2]:
         take_direct(*stage)
     for stage in GP[9:12]:
         relay(*stage)
     for stage in GP[0:6]:
         take_corner(*stage)
-    for stage in DP[4:6]:
+    for stage in DP[2:6]:
         take_direct(*stage)
     for stage in GP[6:9]:
         take_corner(*stage)
     share(1)
-    for stage in DP[6:8]:
+    for stage in DP[6:10]:
         take_direct(*stage)
     for stage in GP[9:12]:
         take_corner(*stage)

time: 39.3 us -> 39.3 us (level)
  no operation moved by 1% of the time
where the time goes in v5:
time: 39.3 us; the launch traced here: 39.2 us
  Pallas kernels  38.6 us (98%)
  other arithmetic  0.56 us (1%)
    pallas_call x1, Pallas kernels, local(): pl.pallas_call(kernel, out_shape=pltpu.VMEM((2, 2, 32), jnp.float32), in_...  38.6 us

profile of v5, /device:TPU:1, one launch (start us, length us, event | category | flops | bytes accessed | tf_op | source)
XLA Modules:
  0.0 39.2 jit_solution(4542103902858037585)
XLA Ops:
  0.0 38.6 %shard_map.46 = f32[2,2,32]{2,1,0:T(2,128)S(1)} custom-call(bf16[12,16,8192]{2,1,0:T(8,128)(2,1)} %bitcast.7, bf16[6,6,128,256]{3,2,1,0:T(8,128)(2,1)} %bitcast.8, bf16[6,16,128]{2,1,0:T(8,128)(2,1)} %bitcast.9, s32[16,128]{1,0:T(8,128)} %mask.1), custom_call_target="tpu_custom_call" | custom-call | tf_op jit(solution)/shard_map/pallas_call | solution.py:258
  38.6 0.6 %add_bitcast_fusion = f32[2,32]{1,0:T(2,128)} fusion(f32[2,2,32]{2,1,0:T(2,128)S(1)} %shard_map.46), kind=kLoop, calls=%fused_computation | loop fusion | flops 64 | bytes 768 | tf_op jit(solution)/shard_map/add | solution.py:292
